TPU v7x, 32 devices: a whole 2x2x4 slice. The times are simulated.
32 devices in a mesh: col: 4 (over z), depth: 8 (over y, x, core).
Axes of the slice: x: 2, y: 2, z: 4, core: 2. Of those that a mesh axis runs over, the one named last changes fastest.
Arguments:
- volume: bfloat16 [128, 256, 512], P('depth', None, 'col'), may hold values from -6 to 6
- tf_index: int32 [128, 256, 512], P('depth', None, 'col'), may hold values from 0 to 255
- tf_table: bfloat16 [4, 256], replicated, may hold values from 0 to 1, as said below
Outputs:
- frame: float32 [4, 256, 512], P(None, 'depth', 'col')
Inputs may be any that keep to these rules, and one draw needn't show every extreme that they name: Rows 0 to 2 of tf_table are positive colours; row 3 is a positive extinction.
All inputs are finite; a program needn't handle non-finite values.
Results may differ from a plain program's by a relative error of at most 0.005.
Values may be sent and summed in bfloat16 or wider, within the bound.
A program may use at most 128 MiB of HBM per device.

v0:
```python
import math

import jax
import jax.numpy as jnp
from jax import lax
from jax.sharding import PartitionSpec as P

light_across = 0.36
light_down = 0.48
light_depth = 0.8


def padded_2(array, sides, width):
    for axis, dim in sides:
        size, length = (lax.axis_size(axis), array.shape[dim])
        up = [(i, (i + 1) % size) for i in range(size - 1)]
        down = [(j, i) for i, j in up]
        last = lax.slice_in_dim(array, length - width, length, axis=dim)
        first = lax.slice_in_dim(array, 0, width, axis=dim)
        before = lax.ppermute(last, axis, up)
        after = lax.ppermute(first, axis, down)
        array = jnp.concatenate([before, array, after], axis=dim)
    return array


def partner(array, axis, apart):
    return lax.ppermute(array, axis, [(i, i ^ 1 << apart) for i in range(lax.axis_size(axis))])


def shading(grad_x, grad_y, grad_z):
    facing = grad_x * light_across + grad_y * light_down + grad_z * light_depth
    return 0.25 + 0.75 * jnp.abs(facing) / jnp.sqrt(
        grad_x * grad_x + grad_y * grad_y + grad_z * grad_z + 1.0
    )


def lookup(tf_index, tf_table):
    flat = tf_index.reshape(-1)
    total = flat.shape[0]
    block = math.gcd(total, 65536)
    entries = tf_table.shape[1]
    low_count = math.gcd(entries, 16)
    high_count = entries // low_count
    folded = tf_table.reshape(4, high_count, low_count).reshape(4 * high_count, low_count)
    low_levels = jnp.arange(low_count, dtype=jnp.int32)[:, None]
    high_levels = jnp.arange(high_count, dtype=jnp.int32)[:, None]

    def one_block(indices):
        low_digit = indices % low_count
        high_digit = indices // low_count
        low_onehot = (low_levels == low_digit[None, :]).astype(jnp.bfloat16)
        partial_rows = jnp.dot(folded, low_onehot, preferred_element_type=jnp.bfloat16)
        partial_rows = partial_rows.reshape(4, high_count, indices.shape[0])
        high_onehot = (high_levels == high_digit[None, :]).astype(jnp.bfloat16)
        return jnp.sum(partial_rows * high_onehot[None], axis=1, dtype=jnp.float32)

    blocks = lax.map(one_block, flat.reshape(total // block, block))
    return jnp.moveaxis(blocks, 1, 0).reshape((4,) + tf_index.shape)


def over(front, back):
    color = front[:3] + jnp.exp(front[3:4]) * back[:3]
    return jnp.concatenate([color, front[3:4] + back[3:4]], 0)


def on_device(volume, tf_index, tf_table):
    depth_cells, rows, columns = volume.shape
    padded = padded_2(volume, (("col", 2), ("depth", 0)), 1)
    padded = jnp.pad(padded, ((0, 0), (1, 1), (0, 0))).astype(jnp.float32)
    grad_x = (padded[1:-1, 1:-1, 2:] - padded[1:-1, 1:-1, :-2]) * 0.5
    grad_y = (padded[1:-1, 2:, 1:-1] - padded[1:-1, :-2, 1:-1]) * 0.5
    grad_z = (padded[2:, 1:-1, 1:-1] - padded[:-2, 1:-1, 1:-1]) * 0.5
    shade = shading(grad_x, grad_y, grad_z)
    looked = lookup(tf_index, tf_table)
    extinction_coefficient = looked[3]
    alpha = -jnp.expm1(-extinction_coefficient)
    inside = jnp.cumsum(extinction_coefficient, axis=0) - extinction_coefficient
    weight = jnp.exp(-inside) * alpha * shade
    color_part = jnp.sum(weight[None] * looked[:3], axis=1)
    optical_part = -jnp.sum(extinction_coefficient, axis=0)
    image = jnp.concatenate([color_part, optical_part[None]], 0)
    count = lax.axis_size("depth")
    sections = count.bit_length() - 1
    block_rows = rows // count
    mine = lax.axis_index("depth")
    region = image.reshape(4, count, block_rows, columns)
    for section in range(sections):
        bit = mine >> section & 1
        halves = region.reshape(4, region.shape[1] // 2, 2, block_rows, columns)
        kept = lax.dynamic_index_in_dim(halves, bit, 2, keepdims=False)
        given = lax.dynamic_index_in_dim(halves, 1 - bit, 2, keepdims=False)
        taken = partner(given, "depth", section)
        front = jnp.where(bit == 0, kept, taken)
        back = jnp.where(bit == 0, taken, kept)
        region = over(front, back)
    final = region.reshape(4, block_rows, columns)
    return jnp.concatenate([final[:3], -jnp.expm1(final[3:4])], 0)


def solution(mesh):
    in_specs = (P("depth", None, "col"), P("depth", None, "col"), P())
    out_specs = P(None, "depth", "col")
    return jax.shard_map(
        on_device, mesh=mesh, in_specs=in_specs, out_specs=out_specs, check_vma=False
    )
```

profile of v0, /device:TPU:0, one launch (start us, length us, event | category | flops | bytes accessed | tf_op | source)
XLA Modules:
  0.0 138.2 jit_solution(15916148283845280847)
XLA Ops:
  0.0 2.1 %fusion.26 = (bf16[16,256,1]{2,1,0:T(8,128)(2,1)S(1)}, bf16[16,256,1]{2,1,0:T(8,128)(2,1)S(1)}) fusion(bf16[16,256,128]{2,1,0:T(8,128)(2,1)} %param.5), kind=kLoop, calls=%fused_computation.72 | loop fusion | bytes 32768 | tf_op jit(solution)/shard_map/slice | solution.py:18
  2.1 0.4 copy.13
  2.5 1.3 collective-permute-start.1
  3.8 0.4 copy.12
  4.2 5.6 %collective-permute-start = (bf16[16,256,1]{1,0,2:T(8,128)(2,1)S(1)}, bf16[16,256,1]{1,0,2:T(8,128)(2,1)S(1)}, u32[]{:S(2)}, u32[]{:S(2)}) collective-permute-start(bf16[16,256,1]{1,0,2:T(8,128)(2,1)S(1)} %copy.12), channel_id=1, source_target_pairs={{0,8},{8,16},{16,24},{1,9},{9,17},{17,25},{2,10},{10,18},{18,26},{... | collective-permute-start | bytes 24584 | tf_op jit(solution)/shard_map/ppermute | solution.py:20
  9.8 2.0 %reshape_reshape.7 = s32[8,65536]{1,0:T(8,128)S(1)} reshape(s32[16,256,128]{2,1,0:T(8,128)} %param.6) | data formatting | bytes 4194304 | tf_op jit(solution)/shard_map/reshape;reshape | solution.py:57
  11.9 69.6 %while.15 = (s32[]{:T(128)}, f32[8,4,65536]{2,1,0:T(4,128)}, s32[8,65536]{1,0:T(8,128)S(1)}, bf16[64,16]{0,1:T(8,128)(2,1)S(1)}, s32[]{:T(128)}) while((s32[]{:T(128)}, f32[8,4,65536]{2,1,0:T(4,128)}, s32[8,65536]{1,0:T(8,128)S(1)}, bf16[64,16]{0,1:T(8,128)(2,1)S(1)}, s32[]{:T(128)}) %tuple.49), condition=%wide.region_2.3_spmd.clone.clone, body=%wide.region_0.2_spmd.clone.clone.sunk | while | flops 151191552 | bytes 9439313 | solution.py:57
  11.9 0.9 and_select_fusion.4
  12.8 1.1 and_select_fusion.5
  13.9 0.3 fusion.33
  14.3 5.3 %convert_reduce_fusion.2 = f32[4,65536]{1,0:T(4,128)S(1)} fusion(bf16[16,65536]{1,0:T(8,128)(2,1)S(1)} %fusion.33, bf16[64,16]{0,1:T(8,128)(2,1)S(1)} %get-tuple-element.195, s32[65536]{0:T(1024)S(1)} %bitcast.50), kind=kOutput, calls=%fused_computation.1.clone.1 | convolution fusion | flops 147587072 | bytes 3409920 | tf_op jit(solution)/shard_map/while/body/eval_jaxpr/dot_general | solution.py:52
  19.6 1.0 bitcast_dynamic-update-slice_fusion.2
  20.6 0.9 and_select_fusion.4
  21.5 1.1 and_select_fusion.5
  22.6 0.3 fusion.33
  23.0 5.3 %convert_reduce_fusion.2 = f32[4,65536]{1,0:T(4,128)S(1)} fusion(bf16[16,65536]{1,0:T(8,128)(2,1)S(1)} %fusion.33, bf16[64,16]{0,1:T(8,128)(2,1)S(1)} %get-tuple-element.195, s32[65536]{0:T(1024)S(1)} %bitcast.50), kind=kOutput, calls=%fused_computation.1.clone.1 | convolution fusion | flops 147587072 | bytes 3409920 | tf_op jit(solution)/shard_map/while/body/eval_jaxpr/dot_general | solution.py:52
  28.2 1.1 bitcast_dynamic-update-slice_fusion.2
  29.3 0.9 and_select_fusion.4
  30.2 1.1 and_select_fusion.5
  31.3 0.3 fusion.33
  31.7 5.3 %convert_reduce_fusion.2 = f32[4,65536]{1,0:T(4,128)S(1)} fusion(bf16[16,65536]{1,0:T(8,128)(2,1)S(1)} %fusion.33, bf16[64,16]{0,1:T(8,128)(2,1)S(1)} %get-tuple-element.195, s32[65536]{0:T(1024)S(1)} %bitcast.50), kind=kOutput, calls=%fused_computation.1.clone.1 | convolution fusion | flops 147587072 | bytes 3409920 | tf_op jit(solution)/shard_map/while/body/eval_jaxpr/dot_general | solution.py:52
  36.9 1.0 bitcast_dynamic-update-slice_fusion.2
  38.0 0.9 and_select_fusion.4
  38.9 1.1 and_select_fusion.5
  40.0 0.3 fusion.33
  40.3 5.3 %convert_reduce_fusion.2 = f32[4,65536]{1,0:T(4,128)S(1)} fusion(bf16[16,65536]{1,0:T(8,128)(2,1)S(1)} %fusion.33, bf16[64,16]{0,1:T(8,128)(2,1)S(1)} %get-tuple-element.195, s32[65536]{0:T(1024)S(1)} %bitcast.50), kind=kOutput, calls=%fused_computation.1.clone.1 | convolution fusion | flops 147587072 | bytes 3409920 | tf_op jit(solution)/shard_map/while/body/eval_jaxpr/dot_general | solution.py:52
  45.6 1.1 bitcast_dynamic-update-slice_fusion.2
  46.7 0.9 and_select_fusion.4
  47.6 1.1 and_select_fusion.5
  48.7 0.3 fusion.33
  49.0 5.3 %convert_reduce_fusion.2 = f32[4,65536]{1,0:T(4,128)S(1)} fusion(bf16[16,65536]{1,0:T(8,128)(2,1)S(1)} %fusion.33, bf16[64,16]{0,1:T(8,128)(2,1)S(1)} %get-tuple-element.195, s32[65536]{0:T(1024)S(1)} %bitcast.50), kind=kOutput, calls=%fused_computation.1.clone.1 | convolution fusion | flops 147587072 | bytes 3409920 | tf_op jit(solution)/shard_map/while/body/eval_jaxpr/dot_general | solution.py:52
  54.3 1.0 bitcast_dynamic-update-slice_fusion.2
  55.4 0.9 and_select_fusion.4
  56.3 1.1 and_select_fusion.5
  57.3 0.3 fusion.33
  57.7 5.3 %convert_reduce_fusion.2 = f32[4,65536]{1,0:T(4,128)S(1)} fusion(bf16[16,65536]{1,0:T(8,128)(2,1)S(1)} %fusion.33, bf16[64,16]{0,1:T(8,128)(2,1)S(1)} %get-tuple-element.195, s32[65536]{0:T(1024)S(1)} %bitcast.50), kind=kOutput, calls=%fused_computation.1.clone.1 | convolution fusion | flops 147587072 | bytes 3409920 | tf_op jit(solution)/shard_map/while/body/eval_jaxpr/dot_general | solution.py:52
  63.0 1.1 bitcast_dynamic-update-slice_fusion.2
  64.1 0.9 and_select_fusion.4
  65.0 1.1 and_select_fusion.5
  66.4 5.3 %convert_reduce_fusion.2 = f32[4,65536]{1,0:T(4,128)S(1)} fusion(bf16[16,65536]{1,0:T(8,128)(2,1)S(1)} %fusion.33, bf16[64,16]{0,1:T(8,128)(2,1)S(1)} %get-tuple-element.195, s32[65536]{0:T(1024)S(1)} %bitcast.50), kind=kOutput, calls=%fused_computation.1.clone.1 | convolution fusion | flops 147587072 | bytes 3409920 | tf_op jit(solution)/shard_map/while/body/eval_jaxpr/dot_general | solution.py:52
  71.7 1.1 bitcast_dynamic-update-slice_fusion.2
  72.8 0.9 and_select_fusion.4
  73.7 1.1 and_select_fusion.5
  75.1 5.3 %convert_reduce_fusion.2 = f32[4,65536]{1,0:T(4,128)S(1)} fusion(bf16[16,65536]{1,0:T(8,128)(2,1)S(1)} %fusion.33, bf16[64,16]{0,1:T(8,128)(2,1)S(1)} %get-tuple-element.195, s32[65536]{0:T(1024)S(1)} %bitcast.50), kind=kOutput, calls=%fused_computation.1.clone.1 | convolution fusion | flops 147587072 | bytes 3409920 | tf_op jit(solution)/shard_map/while/body/eval_jaxpr/dot_general | solution.py:52
  80.4 1.1 bitcast_dynamic-update-slice_fusion.2
  81.5 5.5 %slice.111 = f32[1,8,65536]{2,0,1:T(1,128)S(1)} slice(f32[4,8,65536]{2,0,1:T(4,128)} %bitcast.55), slice={[3:4], [0:8], [0:65536]} | slice | bytes 4194304 | tf_op jit(solution)/shard_map/slice | solution.py:75
  87.0 1.4 %copy.10 = bf16[16,256,1]{2,1,0:T(8,128)(2,1)} copy(bf16[16,256,1]{1,0,2:T(8,128)(2,1)S(1)} %collective-permute-done.1) | data formatting | bytes 16384 | tf_op jit(solution)/shard_map/ppermute | solution.py:21
  88.4 1.4 %copy.9 = bf16[16,256,1]{2,1,0:T(8,128)(2,1)} copy(bf16[16,256,1]{1,0,2:T(8,128)(2,1)S(1)} %collective-permute-done) | data formatting | bytes 16384 | tf_op jit(solution)/shard_map/ppermute | solution.py:20
  89.8 1.7 %pad_maximum_fusion.3 = (bf16[1,256,130]{2,1,0:T(8,128)(2,1)S(1)}, bf16[1,256,130]{2,1,0:T(8,128)(2,1)}) fusion(bf16[16,256,1]{2,1,0:T(8,128)(2,1)} %copy.10, bf16[16,256,128]{2,1,0:T(8,128)(2,1)S(1)} %copy-done, bf16[16,256,1]{2,1,0:T(8,128)(2,1)} %copy.9), kind=kLoop, calls=%fused_computation.46 | loop fusion | flops 399360 | bytes 1198080 | tf_op jit(solution)/shard_map/slice | solution.py:18
  91.6 1.3 collective-permute-start.3
  92.9 3.2 %collective-permute-start.2 = (bf16[1,256,130]{2,1,0:T(8,128)(2,1)S(1)}, bf16[1,256,130]{2,1,0:T(8,128)(2,1)S(1)}, u32[]{:S(2)}, u32[]{:S(2)}) collective-permute-start(bf16[1,256,130]{2,1,0:T(8,128)(2,1)S(1)} %get-tuple-element.135), channel_id=1, source_target_pairs={{0,1},{1,2},{2,3},{3,4},{4,5},{5,6},{6,7},{8,9},{9,10},{10,11},{11... | collective-permute-start | bytes 199688 | tf_op jit(solution)/shard_map/ppermute | solution.py:20
  96.1 1.4 %fusion.27 = f32[16,256,128]{2,1,0:T(8,128)} fusion(f32[16,256,128]{2,1,0:T(8,128)S(1)} %bitcast.53), kind=kOutput, calls=%fused_computation.73 | output fusion | flops 7864320 | bytes 4194304 | tf_op jit(solution)/shard_map/jit(cumsum)/reduce_window_sum | solution.py:77
  97.5 9.7 %copy.11 = f32[3,8,65536]{2,1,0:T(8,128)} copy(f32[3,8,65536]{2,0,1:T(4,128)} %bitcast.56) | data formatting | bytes 12582912 | tf_op jit(solution)/shard_map/slice | solution.py:79
  107.2 6.7 %slice.97 = f32[3,16,256,128]{3,2,1,0:T(8,128)} reshape(f32[3,8,65536]{2,1,0:T(8,128)} %copy.11) | data formatting | bytes 12582912 | tf_op jit(solution)/shard_map/slice | solution.py:79
  114.0 4.9 %fusion.6 = f32[18,258,130]{2,1,0:T(8,128)S(1)} fusion(bf16[1,256,130]{2,1,0:T(8,128)(2,1)S(1)} %collective-permute-done.3, bf16[1,256,130]{2,1,0:T(8,128)(2,1)S(1)} %collective-permute-done.2, bf16[16,256,1]{2,1,0:T(8,128)(2,1)} %copy.10, bf16[16,256,128]{2,1,0:T(8,128)(2,1)S(1)} %copy-done, bf16[16,256,1]{2,1,0:T(8,128)(2,1)} %copy.9), kind=kLoop, calls=%fused_computation.18 | loop fusion | flops 10866960 | bytes 3612960 | tf_op jit(solution)/shard_map/convert_element_type | solution.py:69
  118.9 4.5 %fusion.25 = (f32[256,128]{1,0:T(8,128)S(1)}, f32[16,256,128]{2,1,0:T(8,128)S(1)}) fusion(f32[16,256,128]{2,1,0:T(8,128)S(1)} %bitcast.54, f32[18,258,130]{2,1,0:T(8,128)S(1)} %fusion.6, f32[16,256,128]{2,1,0:T(8,128)S(1)} %copy-done.1), kind=kLoop, calls=%fused_computation.71 | loop fusion | flops 14647296 | bytes 19005440 | tf_op jit(solution)/shard_map/reduce_sum | solution.py:80
  123.4 0.8 multiply_reduce_fusion
  124.2 1.6 %collective-permute-start.4 = (f32[4,4,32,128]{3,2,1,0:T(8,128)S(1)}, f32[4,4,32,128]{3,2,1,0:T(8,128)S(1)}, u32[]{:S(2)}, u32[]{:S(2)}) collective-permute-start(f32[4,4,32,128]{3,2,1,0:T(8,128)S(1)} %fusion.13), channel_id=1, source_target_pairs={{0,1},{1,0},{2,3},{3,2},{4,5},{5,4},{6,7},{7,6},{8,9},{9,8},{10,11... | collective-permute-start | bytes 786440 | tf_op jit(solution)/shard_map/ppermute | solution.py:27
  125.8 1.2 collective-permute-done.4
  127.2 1.9 %collective-permute-start.5 = (f32[4,2,32,128]{3,2,1,0:T(8,128)S(1)}, f32[4,2,32,128]{3,2,1,0:T(8,128)S(1)}, u32[]{:S(2)}, u32[]{:S(2)}) collective-permute-start(f32[4,2,32,128]{3,2,1,0:T(8,128)S(1)} %dynamic-slice_bitcast_fusion), channel_id=1, source_target_pairs={{0,2},{1,3},{2,0},{3,1},{4,6},{5,7},{6,4},{7,5},{8,10},{9,11},{10,... | collective-permute-start | bytes 393224 | tf_op jit(solution)/shard_map/ppermute | solution.py:27
  129.0 4.0 %collective-permute-done.5 = f32[4,2,32,128]{3,2,1,0:T(8,128)S(1)} collective-permute-done((f32[4,2,32,128]{3,2,1,0:T(8,128)S(1)}, f32[4,2,32,128]{3,2,1,0:T(8,128)S(1)}, u32[]{:S(2)}, u32[]{:S(2)}) %collective-permute-start.5) | collective-permute-done | bytes 131104 | tf_op jit(solution)/shard_map/ppermute | solution.py:27
  133.2 1.5 %collective-permute-start.6 = (f32[4,1,32,128]{3,2,1,0:T(8,128)S(1)}, f32[4,1,32,128]{3,2,1,0:T(8,128)S(1)}, u32[]{:S(2)}, u32[]{:S(2)}) collective-permute-start(f32[4,1,32,128]{3,2,1,0:T(8,128)S(1)} %fusion.18), channel_id=1, source_target_pairs={{0,4},{1,5},{2,6},{3,7},{4,0},{5,1},{6,2},{7,3},{8,12},{9,13},{10,... | collective-permute-start | bytes 196616 | tf_op jit(solution)/shard_map/ppermute | solution.py:27
  134.7 2.8 %collective-permute-done.6 = f32[4,1,32,128]{3,2,1,0:T(8,128)S(1)} collective-permute-done((f32[4,1,32,128]{3,2,1,0:T(8,128)S(1)}, f32[4,1,32,128]{3,2,1,0:T(8,128)S(1)}, u32[]{:S(2)}, u32[]{:S(2)}) %collective-permute-start.6) | collective-permute-done | bytes 65568 | tf_op jit(solution)/shard_map/ppermute | solution.py:27
  137.6 0.6 pad_maximum_fusion.4
  (34 shorter events, 1.2 us)
Async XLA Ops:
  2.5 84.5 %collective-permute-start.1 = (bf16[16,256,1]{1,0,2:T(8,128)(2,1)S(1)}, bf16[16,256,1]{1,0,2:T(8,128)(2,1)S(1)}, u32[]{:S(2)}, u32[]{:S(2)}) collective-permute-start(bf16[16,256,1]{1,0,2:T(8,128)(2,1)S(1)} %copy.13), channel_id=1, source_target_pairs={{8,0},{16,8},{24,16},{9,1},{17,9},{25,17},{10,2},{18,10},{26,18},{... | collective-permute-start | bytes 24584 | tf_op jit(solution)/shard_map/ppermute | solution.py:21
  4.2 84.2 %collective-permute-start = (bf16[16,256,1]{1,0,2:T(8,128)(2,1)S(1)}, bf16[16,256,1]{1,0,2:T(8,128)(2,1)S(1)}, u32[]{:S(2)}, u32[]{:S(2)}) collective-permute-start(bf16[16,256,1]{1,0,2:T(8,128)(2,1)S(1)} %copy.12), channel_id=1, source_target_pairs={{0,8},{8,16},{16,24},{1,9},{9,17},{17,25},{2,10},{10,18},{18,26},{... | collective-permute-start | bytes 24584 | tf_op jit(solution)/shard_map/ppermute | solution.py:20
  9.8 2.0 %copy-start.2 = (bf16[4,256]{1,0:T(4,128)(2,1)S(1)}, bf16[4,256]{1,0:T(4,128)(2,1)}, u32[]{:S(2)}) copy-start(bf16[4,256]{1,0:T(4,128)(2,1)} %param.7) | copy-start | bytes 6148
  87.0 2.8 %copy-start = (bf16[16,256,128]{2,1,0:T(8,128)(2,1)S(1)}, bf16[16,256,128]{2,1,0:T(8,128)(2,1)}, u32[]{:S(2)}) copy-start(bf16[16,256,128]{2,1,0:T(8,128)(2,1)} %param.5) | copy-start | bytes 3145732
  91.6 22.4 %collective-permute-start.3 = (bf16[1,256,130]{2,1,0:T(8,128)(2,1)}, bf16[1,256,130]{2,1,0:T(8,128)(2,1)S(1)}, u32[]{:S(2)}, u32[]{:S(2)}) collective-permute-start(bf16[1,256,130]{2,1,0:T(8,128)(2,1)} %get-tuple-element.136), channel_id=1, source_target_pairs={{1,0},{2,1},{3,2},{4,3},{5,4},{6,5},{7,6},{9,8},{10,9},{11,10},{12... | collective-permute-start | bytes 199688 | tf_op jit(solution)/shard_map/ppermute | solution.py:21
  92.9 21.1 %collective-permute-start.2 = (bf16[1,256,130]{2,1,0:T(8,128)(2,1)S(1)}, bf16[1,256,130]{2,1,0:T(8,128)(2,1)S(1)}, u32[]{:S(2)}, u32[]{:S(2)}) collective-permute-start(bf16[1,256,130]{2,1,0:T(8,128)(2,1)S(1)} %get-tuple-element.135), channel_id=1, source_target_pairs={{0,1},{1,2},{2,3},{3,4},{4,5},{5,6},{6,7},{8,9},{9,10},{10,11},{11... | collective-permute-start | bytes 199688 | tf_op jit(solution)/shard_map/ppermute | solution.py:20
  114.0 4.9 %copy-start.1 = (f32[16,256,128]{2,1,0:T(8,128)S(1)}, f32[16,256,128]{2,1,0:T(8,128)}, u32[]{:S(2)}) copy-start(f32[16,256,128]{2,1,0:T(8,128)} %fusion.27) | copy-start | bytes 6291460
  114.0 9.4 %slice-start = ((s8[6291456]{0:T(1024)(128)(4,1)}), s8[4194304]{0:T(1024)(128)(4,1)S(1)}, s32[]{:S(2)}) async-start(s8[6291456]{0:T(1024)(128)(4,1)} %bitcast.51), calls=%async_computation | async-start | bytes 8388608
  118.9 4.5 %slice-start.1 = ((s8[6291456]{0:T(1024)(128)(4,1)}), s8[2097152]{0:T(1024)(128)(4,1)S(1)}, s32[]{:S(2)}) async-start(s8[6291456]{0:T(1024)(128)(4,1)} %bitcast.51), calls=%async_computation.1 | async-start | bytes 4194304
  124.2 2.8 %collective-permute-start.4 = (f32[4,4,32,128]{3,2,1,0:T(8,128)S(1)}, f32[4,4,32,128]{3,2,1,0:T(8,128)S(1)}, u32[]{:S(2)}, u32[]{:S(2)}) collective-permute-start(f32[4,4,32,128]{3,2,1,0:T(8,128)S(1)} %fusion.13), channel_id=1, source_target_pairs={{0,1},{1,0},{2,3},{3,2},{4,5},{5,4},{6,7},{7,6},{8,9},{9,8},{10,11... | collective-permute-start | bytes 786440 | tf_op jit(solution)/shard_map/ppermute | solution.py:27
  127.2 5.9 %collective-permute-start.5 = (f32[4,2,32,128]{3,2,1,0:T(8,128)S(1)}, f32[4,2,32,128]{3,2,1,0:T(8,128)S(1)}, u32[]{:S(2)}, u32[]{:S(2)}) collective-permute-start(f32[4,2,32,128]{3,2,1,0:T(8,128)S(1)} %dynamic-slice_bitcast_fusion), channel_id=1, source_target_pairs={{0,2},{1,3},{2,0},{3,1},{4,6},{5,7},{6,4},{7,5},{8,10},{9,11},{10,... | collective-permute-start | bytes 393224 | tf_op jit(solution)/shard_map/ppermute | solution.py:27
  133.2 4.3 %collective-permute-start.6 = (f32[4,1,32,128]{3,2,1,0:T(8,128)S(1)}, f32[4,1,32,128]{3,2,1,0:T(8,128)S(1)}, u32[]{:S(2)}, u32[]{:S(2)}) collective-permute-start(f32[4,1,32,128]{3,2,1,0:T(8,128)S(1)} %fusion.18), channel_id=1, source_target_pairs={{0,4},{1,5},{2,6},{3,7},{4,0},{5,1},{6,2},{7,3},{8,12},{9,13},{10,... | collective-permute-start | bytes 196616 | tf_op jit(solution)/shard_map/ppermute | solution.py:27
where the time goes:
time: 139 us; the launch traced here: 138 us
  matrix products  42.3 us (30%)
  local copies, waits for them, and re-layouts  38.3 us (28%)
  other arithmetic  32.8 us (24%)
  starting transfers between devices  16.3 us (12%)
  waiting for transfers between devices  8 us (6%)
    dot_general x8, matrix products, one_block(): jnp.dot(folded, low_onehot, preferred_element_type=jnp.bfloat16)  42.3 us
    slice x2, local copies, waits for them, and re-layouts, on_device(): color_part = jnp.sum(weight[None] * looked[:3], axis=1)  16.4 us
    ppermute x2, starting transfers between devices, padded_2(): before = lax.ppermute(last, axis, up)  8.77 us
    select_n x8, other arithmetic, one_block(): high_digit = indices // low_count  8.76 us
    dynamic_update_slice x8, local copies, waits for them, and re-layouts, lookup(): blocks = lax.map(one_block, flat.reshape(total // block, block))  8.5 us
    ppermute x3, waiting for transfers between devices, partner(): lax.ppermute(array, axis, [(i, i ^ 1 << apart) for i in range(lax.axis_si...  7.99 us
    select_n x8, other arithmetic, one_block(): low_digit = indices % low_count  7.12 us
    slice x1, local copies, waits for them, and re-layouts, on_device(): extinction_coefficient = looked[3]  5.54 us
  transfers between devices with their start and end apart: 7, of which 3 were waited for; matrix products, arithmetic and copies ran while one was open for 70% of the time, Pallas kernels for 0%

commit v1 on v0

v1 whole, which is shorter than its diff:
```python
import functools

import jax
import jax.numpy as jnp
from jax import lax
from jax.experimental import pallas as pl
from jax.experimental.pallas import tpu as pltpu
from jax.sharding import PartitionSpec as P

LIGHT = (0.75 * 0.36, 0.75 * 0.48, 0.75 * 0.8)
LOG2E = 1.4426950408889634
LN2 = 0.6931471805599453
PAD = 8


def one_minus_exp(x):
    series = x * (1.0 - x * (0.5 - x * (1.0 / 6.0 - x * (1.0 / 24.0 - x * (1.0 / 120.0)))))
    return jnp.where(x < 0.125, series, 1.0 - jnp.exp(-x))


def kernel(n, vol, idx, table, zlo, zhi, hx, out, fvol, dx, part, recv, send_sem, recv_sem):
    depth, rows, cols = vol.shape
    rb = rows // n
    me = lax.axis_index("depth")

    barrier = pltpu.get_barrier_semaphore()

    def greet(k, c):
        pl.semaphore_signal(barrier, inc=1, device_id={"depth": lax.rem(me + 1 + k, n)},
                            device_id_type=pl.DeviceIdType.MESH)
        return c

    lax.fori_loop(0, n - 1, greet, 0)

    r_i = lax.broadcasted_iota(jnp.int32, (cols, cols), 0)
    c_i = lax.broadcasted_iota(jnp.int32, (cols, cols), 1)
    diff = jnp.where(r_i == c_i + 1, 1.0, 0.0) - jnp.where(r_i == c_i - 1, 1.0, 0.0)
    diff = diff.astype(jnp.bfloat16)
    zero = jnp.zeros((PAD, cols), jnp.float32)
    halo = hx[...]

    def stage(z, c):
        v = vol[z]
        fvol[z + 1, :PAD] = zero
        fvol[z + 1, PAD + rows:] = zero
        fvol[z + 1, PAD:PAD + rows] = v.astype(jnp.float32)
        edge = jnp.where((c_i == cols - 1) & (r_i == depth + z), 1.0, 0.0)
        edge = edge - jnp.where((c_i == 0) & (r_i == z), 1.0, 0.0)
        weights = jnp.concatenate([diff, edge.astype(jnp.bfloat16)], 0)
        both = jnp.concatenate([v, halo], 1)
        dx[z] = jnp.dot(both, weights, preferred_element_type=jnp.float32)
        return c

    lax.fori_loop(0, depth, stage, 0)
    fvol[0, PAD:PAD + rows] = zlo[...].astype(jnp.float32)
    fvol[depth + 1, PAD:PAD + rows] = zhi[...].astype(jnp.float32)

    entries = table[...].astype(jnp.float32)
    sigma = entries[3:4]
    alpha = one_minus_exp(sigma)
    tables = [entries[c:c + 1] * alpha for c in range(3)] + [sigma * -LOG2E]
    sub = 8
    low = [jnp.broadcast_to(t[:, :128], (sub, 128)) for t in tables]
    high = [jnp.broadcast_to(t[:, 128:], (sub, 128)) for t in tables]

    def block(r0):
        def step(z, carry):
            acc0, acc1, acc2, s = carry
            at = pl.multiple_of(PAD + r0, 8)
            gx = dx[z, pl.ds(pl.multiple_of(r0, 8), sub)]
            gy = fvol[z + 1, pl.ds(at + 1, sub)] - fvol[z + 1, pl.ds(at - 1, sub)]
            gz = fvol[z + 2, pl.ds(at, sub)] - fvol[z, pl.ds(at, sub)]
            facing = gx * LIGHT[0] + gy * LIGHT[1] + gz * LIGHT[2]
            inv = lax.rsqrt(gx * gx + gy * gy + (gz * gz + 4.0))
            shade = 0.25 + jnp.abs(facing) * inv
            label = idx[z, pl.ds(pl.multiple_of(r0, 8), sub)]
            in_low = label < 128
            lane = label & 127
            look = [jnp.where(in_low, jnp.take_along_axis(lo, lane, axis=1),
                              jnp.take_along_axis(hi, lane, axis=1))
                    for lo, hi in zip(low, high)]
            w = jnp.exp2(s) * shade
            return (acc0 + w * look[0], acc1 + w * look[1], acc2 + w * look[2], s + look[3])

        init = tuple(jnp.zeros((sub, cols), jnp.float32) for _ in range(4))
        return lax.fori_loop(0, depth, step, init, unroll=True)

    def compute(d):
        tiles = [block(d * rb + sub * i) for i in range(rb // sub)]
        return jnp.concatenate([t[c] for c in range(4) for t in tiles], 0).astype(jnp.bfloat16)

    def copy(k):
        return pltpu.make_async_remote_copy(
            src_ref=part.at[k], dst_ref=recv.at[k],
            send_sem=send_sem.at[k], recv_sem=recv_sem.at[k],
            device_id={"depth": lax.rem(me + 1 + k, n)},
            device_id_type=pl.DeviceIdType.MESH)

    pl.semaphore_wait(barrier, n - 1)

    def work(k, c):
        part[k] = compute(lax.rem(me + 1 + k, n))
        copy(k).start()
        return c

    lax.fori_loop(0, n - 1, work, 0)
    recv[n - 1] = compute(me)

    def arrive(k, c):
        copy(k).wait()
        return c

    lax.fori_loop(0, n - 1, arrive, 0)

    def over(j, carry):
        color, s = carry
        piece = recv[lax.rem(me - j - 1 + 2 * n, n)].astype(jnp.float32)
        t = jnp.exp2(s)
        color = tuple(color[c] + t * piece[c * rb:(c + 1) * rb] for c in range(3))
        return color, s + piece[3 * rb:]

    init = jnp.zeros((rb, cols), jnp.float32)
    color, s = lax.fori_loop(0, n, over, ((init,) * 3, init))
    for c in range(3):
        out[c] = color[c]
    out[3] = one_minus_exp(s * -LN2)


def on_device(volume, tf_index, tf_table):
    depth, rows, cols = volume.shape
    n = lax.axis_size("depth")
    across = lax.axis_size("col")
    up = lambda m: [(i, i + 1) for i in range(m - 1)]
    down = lambda m: [(i + 1, i) for i in range(m - 1)]
    zlo = lax.ppermute(volume[-1], "depth", up(n))
    zhi = lax.ppermute(volume[0], "depth", down(n))
    left = lax.ppermute(volume[:, :, -1], "col", up(across))
    right = lax.ppermute(volume[:, :, 0], "col", down(across))
    hx = jnp.concatenate([left, right], 0).T
    hx = jnp.pad(hx, ((0, 0), (0, cols - 2 * depth)))
    vm = pl.BlockSpec(memory_space=pltpu.VMEM)
    rb = rows // n
    return pl.pallas_call(
        functools.partial(kernel, n),
        out_shape=jax.ShapeDtypeStruct((4, rb, cols), jnp.float32),
        in_specs=[vm] * 6,
        out_specs=vm,
        scratch_shapes=[
            pltpu.VMEM((depth + 2, rows + 2 * PAD, cols), jnp.float32),
            pltpu.VMEM((depth, rows, cols), jnp.float32),
            pltpu.VMEM((n, 4 * rb, cols), jnp.bfloat16),
            pltpu.VMEM((n, 4 * rb, cols), jnp.bfloat16),
            pltpu.SemaphoreType.DMA((n - 1,)),
            pltpu.SemaphoreType.DMA((n - 1,)),
        ],
        compiler_params=pltpu.CompilerParams(
            collective_id=0, has_side_effects=True, vmem_limit_bytes=32 * 1024 * 1024),
    )(volume, tf_index, tf_table, zlo, zhi, hx)


def solution(mesh):
    in_specs = (P("depth", None, "col"), P("depth", None, "col"), P())
    out_specs = P(None, "depth", "col")
    return jax.shard_map(
        on_device, mesh=mesh, in_specs=in_specs, out_specs=out_specs, check_vma=False
    )
```

time: 139 us -> 34.4 us (0.25)
  matrix products: 42.3 us -> 0 us
  other arithmetic: 32.8 us -> 0.01 us
  local copies, waits for them, and re-layouts: 38.3 us -> 7.49 us
  Pallas kernels: 0 us -> 14.1 us
  starting transfers between devices: 16.3 us -> 8.97 us
  waiting for transfers between devices: 8 us -> 3.24 us
    dot_general x8 -> x0, matrix products: 42.3 us -> none  [one_block(): jnp.dot(folded, low_onehot, preferred_element_type=jnp.bfloat16)]
    slice x4 -> x1, local copies, waits for them, and re-layouts: 24.1 us -> 3.42 us  [on_device(): left = lax.ppermute(volume[:, :, -1], 'col', up(across))]
    select_n x19 -> x0, other arithmetic: 16 us -> none  [the longest x8 8.76 us: one_block(): high_digit = indices // low_count]
    pallas_call x0 -> x1, Pallas kernels: none -> 14.1 us  [on_device(): pl.pallas_call(functools.partial(kernel, n), out_shape=jax.ShapeDtypeStru...]
    dynamic_update_slice x8 -> x0, local copies, waits for them, and re-layouts: 8.5 us -> none  [lookup(): blocks = lax.map(one_block, flat.reshape(total // block, block))]
    convert_element_type x9 -> x0, other arithmetic: 7.61 us -> none  [the longest x1 4.87 us: on_device(): padded = jnp.pad(padded, ((0, 0), (1, 1), (0, 0))).astype(jnp.float32)]
    ppermute x7 -> x4, starting transfers between devices: 16.3 us -> 8.97 us  [the longest x1 4.93 us: on_device(): left = lax.ppermute(volume[:, :, -1], 'col', up(across))]
    reduce_sum x2 -> x0, other arithmetic: 5.23 us -> none  [the longest x1 4.47 us: on_device(): optical_part = -jnp.sum(extinction_coefficient, axis=0)]
  transfers between devices with their start and end apart: 7 -> 4, of which waited for: 3 -> 2; matrix products, arithmetic and copies ran while one was open for 70% -> 5% of each run, Pallas kernels for 0% -> 0%
where the time goes in v1:
time: 34.4 us; the launch traced here: 33.9 us
  Pallas kernels  14.1 us (41%)
  starting transfers between devices  8.97 us (26%)
  local copies, waits for them, and re-layouts  7.49 us (22%)
  waiting for transfers between devices  3.24 us (9%)
    pallas_call x1, Pallas kernels, on_device(): pl.pallas_call(functools.partial(kernel, n), out_shape=jax.ShapeDtypeStru...  14.1 us
    ppermute x1, starting transfers between devices, on_device(): left = lax.ppermute(volume[:, :, -1], 'col', up(across))  4.93 us
    unnamed x9, local copies, waits for them, and re-layouts  3.91 us
    slice x1, local copies, waits for them, and re-layouts, on_device(): left = lax.ppermute(volume[:, :, -1], 'col', up(across))  3.42 us
    ppermute x1, waiting for transfers between devices, on_device(): zhi = lax.ppermute(volume[0], 'depth', down(n))  1.8 us
    ppermute x1, starting transfers between devices, on_device(): zlo = lax.ppermute(volume[-1], 'depth', up(n))  1.46 us
    ppermute x1, waiting for transfers between devices, on_device(): right = lax.ppermute(volume[:, :, 0], 'col', down(across))  1.44 us
    ppermute x1, starting transfers between devices, on_device(): zhi = lax.ppermute(volume[0], 'depth', down(n))  1.29 us
  transfers between devices with their start and end apart: 4, of which 2 were waited for; matrix products, arithmetic and copies ran while one was open for 5% of the time, Pallas kernels for 0%

profile of v1, /device:TPU:0, one launch (start us, length us, event | category | flops | bytes accessed | tf_op | source)
XLA Modules:
  0.0 33.9 jit_solution(17065784228722471846)
XLA Ops:
  0.0 0.0 copy-start.1
  0.0 3.4 %fusion = (bf16[16,256,1]{2,1,0:T(8,128)(2,1)}, bf16[16,256,1]{2,1,0:T(8,128)(2,1)}) fusion(bf16[16,256,128]{2,1,0:T(8,128)(2,1)} %vol.1), kind=kLoop, calls=%fused_computation.3 | loop fusion | bytes 32768 | tf_op jit(solution)/shard_map/slice | solution.py:137
  3.4 0.0 copy-start
  3.4 0.0 copy-start.2
  3.4 1.7 %copy.9 = bf16[16,256,1]{1,0,2:T(8,128)(2,1)S(1)} copy(bf16[16,256,1]{2,1,0:T(8,128)(2,1)} %get-tuple-element.5) | data formatting | bytes 16384
  5.1 4.9 %collective-permute-start.2 = (bf16[16,256]{1,0:T(8,128)(2,1)S(1)}, bf16[16,256]{1,0:T(8,128)(2,1)S(1)}, u32[]{:S(2)}, u32[]{:S(2)}) collective-permute-start(bf16[16,256]{1,0:T(8,128)(2,1)S(1)} %bitcast.8), channel_id=1, source_target_pairs={{0,8},{8,16},{16,24},{1,9},{9,17},{17,25},{2,10},{10,18},{18,26},{... | collective-permute-start | bytes 24584 | tf_op jit(solution)/shard_map/ppermute | solution.py:137
  10.0 1.6 %copy.10 = bf16[16,256,1]{1,0,2:T(8,128)(2,1)S(1)} copy(bf16[16,256,1]{2,1,0:T(8,128)(2,1)} %get-tuple-element.6) | data formatting | bytes 16384
  11.6 1.3 %collective-permute-start.3 = (bf16[16,256]{1,0:T(8,128)(2,1)S(1)}, bf16[16,256]{1,0:T(8,128)(2,1)S(1)}, u32[]{:S(2)}, u32[]{:S(2)}) collective-permute-start(bf16[16,256]{1,0:T(8,128)(2,1)S(1)} %bitcast.9), channel_id=1, source_target_pairs={{8,0},{16,8},{24,16},{9,1},{17,9},{25,17},{10,2},{18,10},{26,18},{... | collective-permute-start | bytes 24584 | tf_op jit(solution)/shard_map/ppermute | solution.py:138
  12.9 0.0 copy-done
  13.0 1.5 %collective-permute-start = (bf16[256,128]{1,0:T(8,128)(2,1)S(1)}, bf16[256,128]{1,0:T(8,128)(2,1)S(1)}, u32[]{:S(2)}, u32[]{:S(2)}) collective-permute-start(bf16[256,128]{1,0:T(8,128)(2,1)S(1)} %get-tuple-element.8), channel_id=1, source_target_pairs={{0,1},{1,2},{2,3},{3,4},{4,5},{5,6},{6,7},{8,9},{9,10},{10,11},{11... | collective-permute-start | bytes 196616 | tf_op jit(solution)/shard_map/ppermute | solution.py:135
  14.4 1.3 %collective-permute-start.1 = (bf16[256,128]{1,0:T(8,128)(2,1)S(1)}, bf16[256,128]{1,0:T(8,128)(2,1)S(1)}, u32[]{:S(2)}, u32[]{:S(2)}) collective-permute-start(bf16[256,128]{1,0:T(8,128)(2,1)S(1)} %get-tuple-element.7), channel_id=1, source_target_pairs={{1,0},{2,1},{3,2},{4,3},{5,4},{6,5},{7,6},{9,8},{10,9},{11,10},{12... | collective-permute-start | bytes 196616 | tf_op jit(solution)/shard_map/ppermute | solution.py:136
  15.7 0.0 collective-permute-done.2
  15.7 1.4 %collective-permute-done.3 = bf16[16,256]{1,0:T(8,128)(2,1)S(1)} collective-permute-done((bf16[16,256]{1,0:T(8,128)(2,1)S(1)}, bf16[16,256]{1,0:T(8,128)(2,1)S(1)}, u32[]{:S(2)}, u32[]{:S(2)}) %collective-permute-start.3) | collective-permute-done | bytes 8224 | tf_op jit(solution)/shard_map/ppermute | solution.py:138
  17.2 0.1 copy.8
  17.3 0.0 collective-permute-done.zlo
  17.3 1.8 %collective-permute-done.1.zhi = bf16[256,128]{1,0:T(8,128)(2,1)S(1)} collective-permute-done((bf16[256,128]{1,0:T(8,128)(2,1)S(1)}, bf16[256,128]{1,0:T(8,128)(2,1)S(1)}, u32[]{:S(2)}, u32[]{:S(2)}) %collective-permute-start.1) | collective-permute-done | bytes 65568 | tf_op jit(solution)/shard_map/ppermute | solution.py:136
  19.1 0.0 copy-done.1
  19.1 0.0 copy-done.2
  19.1 14.1 %shard_map.37 = f32[4,32,128]{2,1,0:T(8,128)S(1)} custom-call(bf16[16,256,128]{2,1,0:T(8,128)(2,1)S(1)} %copy-done, s32[16,256,128]{2,1,0:T(8,128)S(1)} %copy-done.1, bf16[4,256]{1,0:T(4,128)(2,1)S(1)} %copy-done.2, bf16[256,128]{1,0:T(8,128)(2,1)S(1)} %collective-permute-done.zlo, bf16[256,128]{1,0:T(8,128)(2,1)S(1)} %collective-permute-done.1.zhi, ...), custom_call_target="tpu_custom_call" | custom-call | tf_op jit(solution)/shard_map/pallas_call | solution.py:143
  33.3 0.6 %copy.12 = f32[4,32,128]{2,1,0:T(8,128)} copy(f32[4,32,128]{2,1,0:T(8,128)S(1)} %shard_map.37) | data formatting | bytes 131072
  (3 shorter events, 0.0 us)
Async XLA Ops:
  0.0 19.1 %copy-start.1 = (s32[16,256,128]{2,1,0:T(8,128)S(1)}, s32[16,256,128]{2,1,0:T(8,128)}, u32[]{:S(2)}) copy-start(s32[16,256,128]{2,1,0:T(8,128)} %idx.1) | copy-start | bytes 6291460
  3.4 9.5 %copy-start = (bf16[16,256,128]{2,1,0:T(8,128)(2,1)S(1)}, bf16[16,256,128]{2,1,0:T(8,128)(2,1)}, u32[]{:S(2)}) copy-start(bf16[16,256,128]{2,1,0:T(8,128)(2,1)} %vol.1) | copy-start | bytes 3145732
  3.4 15.7 %copy-start.2 = (bf16[4,256]{1,0:T(4,128)(2,1)S(1)}, bf16[4,256]{1,0:T(4,128)(2,1)}, u32[]{:S(2)}) copy-start(bf16[4,256]{1,0:T(4,128)(2,1)} %table.1) | copy-start | bytes 6148
  5.1 10.6 %collective-permute-start.2 = (bf16[16,256]{1,0:T(8,128)(2,1)S(1)}, bf16[16,256]{1,0:T(8,128)(2,1)S(1)}, u32[]{:S(2)}, u32[]{:S(2)}) collective-permute-start(bf16[16,256]{1,0:T(8,128)(2,1)S(1)} %bitcast.8), channel_id=1, source_target_pairs={{0,8},{8,16},{16,24},{1,9},{9,17},{17,25},{2,10},{10,18},{18,26},{... | collective-permute-start | bytes 24584 | tf_op jit(solution)/shard_map/ppermute | solution.py:137
  11.6 5.5 %collective-permute-start.3 = (bf16[16,256]{1,0:T(8,128)(2,1)S(1)}, bf16[16,256]{1,0:T(8,128)(2,1)S(1)}, u32[]{:S(2)}, u32[]{:S(2)}) collective-permute-start(bf16[16,256]{1,0:T(8,128)(2,1)S(1)} %bitcast.9), channel_id=1, source_target_pairs={{8,0},{16,8},{24,16},{9,1},{17,9},{25,17},{10,2},{18,10},{26,18},{... | collective-permute-start | bytes 24584 | tf_op jit(solution)/shard_map/ppermute | solution.py:138
  13.0 4.4 %collective-permute-start = (bf16[256,128]{1,0:T(8,128)(2,1)S(1)}, bf16[256,128]{1,0:T(8,128)(2,1)S(1)}, u32[]{:S(2)}, u32[]{:S(2)}) collective-permute-start(bf16[256,128]{1,0:T(8,128)(2,1)S(1)} %get-tuple-element.8), channel_id=1, source_target_pairs={{0,1},{1,2},{2,3},{3,4},{4,5},{5,6},{6,7},{8,9},{9,10},{10,11},{11... | collective-permute-start | bytes 196616 | tf_op jit(solution)/shard_map/ppermute | solution.py:135
  14.4 4.7 %collective-permute-start.1 = (bf16[256,128]{1,0:T(8,128)(2,1)S(1)}, bf16[256,128]{1,0:T(8,128)(2,1)S(1)}, u32[]{:S(2)}, u32[]{:S(2)}) collective-permute-start(bf16[256,128]{1,0:T(8,128)(2,1)S(1)} %get-tuple-element.7), channel_id=1, source_target_pairs={{1,0},{2,1},{3,2},{4,3},{5,4},{6,5},{7,6},{9,8},{10,9},{11,10},{12... | collective-permute-start | bytes 196616 | tf_op jit(solution)/shard_map/ppermute | solution.py:136

commit v2 on v1

--- a/solution.py
+++ b/solution.py
@@ -18,10 +18,12 @@
     return jnp.where(x < 0.125, series, 1.0 - jnp.exp(-x))
 
 
-def kernel(n, vol, idx, table, zlo, zhi, hx, out, fvol, dx, part, recv, send_sem, recv_sem):
+def kernel(n, m, vol, idx, table, out, fvol, dx, part, recv, edge, zlo, zhi, from_left, from_right,
+           send_sem, recv_sem, halo_send, halo_recv):
     depth, rows, cols = vol.shape
     rb = rows // n
     me = lax.axis_index("depth")
+    mine = lax.axis_index("col")
 
     barrier = pltpu.get_barrier_semaphore()
 
@@ -31,27 +33,78 @@
         return c
 
     lax.fori_loop(0, n - 1, greet, 0)
+    for there, side in ((mine > 0, -1), (mine < m - 1, 1)):
+        @pl.when(there)
+        def _():
+            pl.semaphore_signal(barrier, inc=1, device_id={"col": mine + side},
+                                device_id_type=pl.DeviceIdType.MESH)
+
+    def halo_copy(k, src, dst, axis, to):
+        return pltpu.make_async_remote_copy(
+            src_ref=src, dst_ref=dst, send_sem=halo_send.at[k], recv_sem=halo_recv.at[k],
+            device_id={axis: to}, device_id_type=pl.DeviceIdType.MESH)
+
+    along_z = ((me > 0, me < n - 1, halo_copy(0, vol.at[0], zhi, "depth", me - 1), zhi),
+               (me < n - 1, me > 0, halo_copy(1, vol.at[depth - 1], zlo, "depth", me + 1), zlo))
+    along_x = ((mine > 0, mine < m - 1, halo_copy(2, edge, from_right, "col", mine - 1), from_right),
+               (mine < m - 1, mine > 0, halo_copy(3, edge, from_left, "col", mine + 1), from_left))
+
+    def send(halos):
+        for sends, _, copy, _ in halos:
+            pl.when(sends)(copy.start)
+
+    def receive(halos):
+        for sends, receives, copy, landed in halos:
+            pl.when(sends)(copy.wait_send)
+            pl.when(receives)(copy.wait_recv)
+
+            @pl.when(jnp.logical_not(receives))
+            def _():
+                landed[...] = jnp.zeros_like(landed)
+
+    neighbours = (mine > 0).astype(jnp.int32) + (mine < m - 1).astype(jnp.int32)
+    pl.semaphore_wait(barrier, n - 1 + neighbours)
+    send(along_z)
 
     r_i = lax.broadcasted_iota(jnp.int32, (cols, cols), 0)
     c_i = lax.broadcasted_iota(jnp.int32, (cols, cols), 1)
     diff = jnp.where(r_i == c_i + 1, 1.0, 0.0) - jnp.where(r_i == c_i - 1, 1.0, 0.0)
     diff = diff.astype(jnp.bfloat16)
     zero = jnp.zeros((PAD, cols), jnp.float32)
-    halo = hx[...]
-
-    def stage(z, c):
+
+    def pick(z, total):
+        at = jnp.where((r_i == cols - 1) & (c_i == z), 1.0, 0.0)
+        at = at + jnp.where((r_i == 0) & (c_i == depth + z), 1.0, 0.0)
+        return total + jnp.dot(vol[z], at.astype(jnp.bfloat16), preferred_element_type=jnp.float32)
+
+    edges = lax.fori_loop(0, depth, pick, jnp.zeros((rows, cols), jnp.float32), unroll=4)
+    edge[...] = edges.astype(jnp.bfloat16)
+    send(along_x)
+
+    def widen(z, c):
         v = vol[z]
         fvol[z + 1, :PAD] = zero
         fvol[z + 1, PAD + rows:] = zero
         fvol[z + 1, PAD:PAD + rows] = v.astype(jnp.float32)
-        edge = jnp.where((c_i == cols - 1) & (r_i == depth + z), 1.0, 0.0)
-        edge = edge - jnp.where((c_i == 0) & (r_i == z), 1.0, 0.0)
-        weights = jnp.concatenate([diff, edge.astype(jnp.bfloat16)], 0)
+        return c
+
+    lax.fori_loop(0, depth, widen, 0, unroll=2)
+    receive(along_x)
+    lane = lax.broadcasted_iota(jnp.int32, (rows, cols), 1)
+    halo = jnp.where(lane < depth, from_left[...].astype(jnp.float32), from_right[...].astype(jnp.float32))
+    halo = halo.astype(jnp.bfloat16)
+
+    def stage(z, c):
+        v = vol[z]
+        ends = jnp.where((c_i == cols - 1) & (r_i == depth + z), 1.0, 0.0)
+        ends = ends - jnp.where((c_i == 0) & (r_i == z), 1.0, 0.0)
+        weights = jnp.concatenate([diff, ends.astype(jnp.bfloat16)], 0)
         both = jnp.concatenate([v, halo], 1)
         dx[z] = jnp.dot(both, weights, preferred_element_type=jnp.float32)
         return c
 
-    lax.fori_loop(0, depth, stage, 0)
+    lax.fori_loop(0, depth, stage, 0, unroll=4)
+    receive(along_z)
     fvol[0, PAD:PAD + rows] = zlo[...].astype(jnp.float32)
     fvol[depth + 1, PAD:PAD + rows] = zhi[...].astype(jnp.float32)
 
@@ -96,8 +149,6 @@
             device_id={"depth": lax.rem(me + 1 + k, n)},
             device_id_type=pl.DeviceIdType.MESH)
 
-    pl.semaphore_wait(barrier, n - 1)
-
     def work(k, c):
         part[k] = compute(lax.rem(me + 1 + k, n))
         copy(k).start()
@@ -129,33 +180,28 @@
 def on_device(volume, tf_index, tf_table):
     depth, rows, cols = volume.shape
     n = lax.axis_size("depth")
-    across = lax.axis_size("col")
-    up = lambda m: [(i, i + 1) for i in range(m - 1)]
-    down = lambda m: [(i + 1, i) for i in range(m - 1)]
-    zlo = lax.ppermute(volume[-1], "depth", up(n))
-    zhi = lax.ppermute(volume[0], "depth", down(n))
-    left = lax.ppermute(volume[:, :, -1], "col", up(across))
-    right = lax.ppermute(volume[:, :, 0], "col", down(across))
-    hx = jnp.concatenate([left, right], 0).T
-    hx = jnp.pad(hx, ((0, 0), (0, cols - 2 * depth)))
+    m = lax.axis_size("col")
     vm = pl.BlockSpec(memory_space=pltpu.VMEM)
     rb = rows // n
     return pl.pallas_call(
-        functools.partial(kernel, n),
+        functools.partial(kernel, n, m),
         out_shape=jax.ShapeDtypeStruct((4, rb, cols), jnp.float32),
-        in_specs=[vm] * 6,
+        in_specs=[vm] * 3,
         out_specs=vm,
         scratch_shapes=[
             pltpu.VMEM((depth + 2, rows + 2 * PAD, cols), jnp.float32),
             pltpu.VMEM((depth, rows, cols), jnp.float32),
             pltpu.VMEM((n, 4 * rb, cols), jnp.bfloat16),
             pltpu.VMEM((n, 4 * rb, cols), jnp.bfloat16),
+            *[pltpu.VMEM((rows, cols), jnp.bfloat16)] * 5,
             pltpu.SemaphoreType.DMA((n - 1,)),
             pltpu.SemaphoreType.DMA((n - 1,)),
+            pltpu.SemaphoreType.DMA((4,)),
+            pltpu.SemaphoreType.DMA((4,)),
         ],
         compiler_params=pltpu.CompilerParams(
             collective_id=0, has_side_effects=True, vmem_limit_bytes=32 * 1024 * 1024),
-    )(volume, tf_index, tf_table, zlo, zhi, hx)
+    )(volume, tf_index, tf_table)
 
 
 def solution(mesh):

time: 34.4 us -> 22.3 us (0.65)
  starting transfers between devices: 8.97 us -> 0 us
  Pallas kernels: 14.1 us -> 17.8 us
  local copies, waits for them, and re-layouts: 7.49 us -> 4.13 us
  waiting for transfers between devices: 3.24 us -> 0 us
    ppermute x4 -> x0, starting transfers between devices: 8.97 us -> none  [the longest x1 4.93 us: on_device(): left = lax.ppermute(volume[:, :, -1], 'col', up(across))]
    pallas_call x1, Pallas kernels: 14.1 us -> 17.8 us  [on_device(): pl.pallas_call(functools.partial(kernel, n, m), out_shape=jax.ShapeDtypeS...]
    slice x1 -> x0, local copies, waits for them, and re-layouts: 3.42 us -> none  [on_device(): left = lax.ppermute(volume[:, :, -1], 'col', up(across))]
    ppermute x4 -> x0, waiting for transfers between devices: 3.24 us -> none  [the longest x1 1.8 us: on_device(): zhi = lax.ppermute(volume[0], 'depth', down(n))]
    unnamed x9 -> x7, local copies, waits for them, and re-layouts: 3.91 us -> 4.13 us
  transfers between devices with their start and end apart: 4 -> 0, of which waited for: 2 -> 0; matrix products, arithmetic and copies ran while one was open for 5% -> 0% of each run, Pallas kernels for 0% -> 0%
where the time goes in v2:
time: 22.3 us; the launch traced here: 22 us
  Pallas kernels  17.8 us (80%)
  local copies, waits for them, and re-layouts  4.13 us (19%)
    pallas_call x1, Pallas kernels, on_device(): pl.pallas_call(functools.partial(kernel, n, m), out_shape=jax.ShapeDtypeS...  17.8 us
    unnamed x7, local copies, waits for them, and re-layouts  4.13 us

profile of v2, /device:TPU:0, one launch (start us, length us, event | category | flops | bytes accessed | tf_op | source)
XLA Modules:
  0.0 22.0 jit_solution(10759424380276876939)
XLA Ops:
  0.0 0.0 copy-start
  0.0 1.6 %copy-done = s32[16,256,128]{2,1,0:T(8,128)S(1)} copy-done((s32[16,256,128]{2,1,0:T(8,128)S(1)}, s32[16,256,128]{2,1,0:T(8,128)}, u32[]{:S(2)}) %copy-start) | copy-done | bytes 2097176
  1.6 0.0 copy-start.1
  1.6 1.2 %copy-done.1 = bf16[16,256,128]{2,1,0:T(8,128)(2,1)S(1)} copy-done((bf16[16,256,128]{2,1,0:T(8,128)(2,1)S(1)}, bf16[16,256,128]{2,1,0:T(8,128)(2,1)}, u32[]{:S(2)}) %copy-start.1) | copy-done | bytes 1048600
  2.8 0.0 copy-start.2
  2.8 0.7 %copy-done.2 = bf16[4,256]{1,0:T(4,128)(2,1)S(1)} copy-done((bf16[4,256]{1,0:T(4,128)(2,1)S(1)}, bf16[4,256]{1,0:T(4,128)(2,1)}, u32[]{:S(2)}) %copy-start.2) | copy-done | bytes 2072
  3.5 17.8 %shard_map.37 = f32[4,32,128]{2,1,0:T(8,128)S(1)} custom-call(bf16[16,256,128]{2,1,0:T(8,128)(2,1)S(1)} %copy-done.1, s32[16,256,128]{2,1,0:T(8,128)S(1)} %copy-done, bf16[4,256]{1,0:T(4,128)(2,1)S(1)} %copy-done.2), custom_call_target="tpu_custom_call" | custom-call | tf_op jit(solution)/shard_map/pallas_call | solution.py:186
  21.3 0.6 %copy.5 = f32[4,32,128]{2,1,0:T(8,128)} copy(f32[4,32,128]{2,1,0:T(8,128)S(1)} %shard_map.37) | data formatting | bytes 131072
Async XLA Ops:
  0.0 1.6 %copy-start = (s32[16,256,128]{2,1,0:T(8,128)S(1)}, s32[16,256,128]{2,1,0:T(8,128)}, u32[]{:S(2)}) copy-start(s32[16,256,128]{2,1,0:T(8,128)} %idx.1) | copy-start | bytes 6291460
  1.6 1.2 %copy-start.1 = (bf16[16,256,128]{2,1,0:T(8,128)(2,1)S(1)}, bf16[16,256,128]{2,1,0:T(8,128)(2,1)}, u32[]{:S(2)}) copy-start(bf16[16,256,128]{2,1,0:T(8,128)(2,1)} %vol.1) | copy-start | bytes 3145732
  2.8 0.7 %copy-start.2 = (bf16[4,256]{1,0:T(4,128)(2,1)S(1)}, bf16[4,256]{1,0:T(4,128)(2,1)}, u32[]{:S(2)}) copy-start(bf16[4,256]{1,0:T(4,128)(2,1)} %table.1) | copy-start | bytes 6148

commit v3 on v2

--- a/solution.py
+++ b/solution.py
@@ -18,12 +18,17 @@
     return jnp.where(x < 0.125, series, 1.0 - jnp.exp(-x))
 
 
-def kernel(n, m, vol, idx, table, out, fvol, dx, part, recv, edge, zlo, zhi, from_left, from_right,
+def kernel(n, m, vol_hbm, idx_hbm, table_hbm, out, vol, idx, table, load_sem, fvol, dx, part, recv, edge, zlo, zhi, from_left, from_right,
            send_sem, recv_sem, halo_send, halo_recv):
     depth, rows, cols = vol.shape
     rb = rows // n
     me = lax.axis_index("depth")
     mine = lax.axis_index("col")
+
+    loads = [pltpu.make_async_copy(src, dst, load_sem.at[i]) for i, (src, dst) in
+             enumerate(((table_hbm, table), (vol_hbm, vol), (idx_hbm, idx)))]
+    for load in loads:
+        load.start()
 
     barrier = pltpu.get_barrier_semaphore()
 
@@ -62,10 +67,32 @@
             def _():
                 landed[...] = jnp.zeros_like(landed)
 
-    neighbours = (mine > 0).astype(jnp.int32) + (mine < m - 1).astype(jnp.int32)
-    pl.semaphore_wait(barrier, n - 1 + neighbours)
-    send(along_z)
-
+    loads[0].wait()
+    entries = table[...].astype(jnp.float32)
+    sigma = entries[3:4]
+    alpha = one_minus_exp(sigma)
+    logs = [jnp.log(jnp.maximum(v, 1.2e-38)) * LOG2E
+            for v in [entries[c:c + 1] * alpha for c in range(3)] + [sigma * LOG2E]]
+    most = [jnp.max(v, axis=1, keepdims=True) for v in logs]
+    least = [jnp.min(v, axis=1, keepdims=True) for v in logs]
+    middle = [0.5 * (a + b) for a, b in zip(most, least)]
+    grain = [jnp.maximum(a - b, 1e-3) * (1.0 / 65532.0) for a, b in zip(most, least)]
+    place = [(v - o) / g for v, o, g in zip(logs, middle, grain)]
+
+    def word(upper, lower):
+        lower = jnp.floor(lower + 0.5)
+        upper = jnp.floor(upper - lower * (1.0 / 65536.0) + 0.5)
+        return upper.astype(jnp.int32) * 65536 + lower.astype(jnp.int32)
+
+    sub = 8
+    words = (word(place[0], place[1]), word(place[2], place[3]))
+    low = [jnp.broadcast_to(t[:, :128], (sub, 128)) for t in words]
+    high = [jnp.broadcast_to(t[:, 128:], (sub, 128)) for t in words]
+    spread = [jnp.broadcast_to(g * (1.0 / 65536.0), (sub, cols)) for g in grain]
+    sigma_middle = jnp.broadcast_to(middle[3], (sub, cols))
+    scale = [jnp.broadcast_to(jnp.exp2(o), (sub, cols)) for o in middle[:3]]
+
+    loads[1].wait()
     r_i = lax.broadcasted_iota(jnp.int32, (cols, cols), 0)
     c_i = lax.broadcasted_iota(jnp.int32, (cols, cols), 1)
     diff = jnp.where(r_i == c_i + 1, 1.0, 0.0) - jnp.where(r_i == c_i - 1, 1.0, 0.0)
@@ -79,6 +106,10 @@
 
     edges = lax.fori_loop(0, depth, pick, jnp.zeros((rows, cols), jnp.float32), unroll=4)
     edge[...] = edges.astype(jnp.bfloat16)
+    neighbours = (mine > 0).astype(jnp.int32) + (mine < m - 1).astype(jnp.int32)
+    pl.semaphore_wait(barrier, n - 1 + neighbours)
+    send(along_z)
+
     send(along_x)
 
     def widen(z, c):
@@ -105,16 +136,9 @@
 
     lax.fori_loop(0, depth, stage, 0, unroll=4)
     receive(along_z)
+    loads[2].wait()
     fvol[0, PAD:PAD + rows] = zlo[...].astype(jnp.float32)
     fvol[depth + 1, PAD:PAD + rows] = zhi[...].astype(jnp.float32)
-
-    entries = table[...].astype(jnp.float32)
-    sigma = entries[3:4]
-    alpha = one_minus_exp(sigma)
-    tables = [entries[c:c + 1] * alpha for c in range(3)] + [sigma * -LOG2E]
-    sub = 8
-    low = [jnp.broadcast_to(t[:, :128], (sub, 128)) for t in tables]
-    high = [jnp.broadcast_to(t[:, 128:], (sub, 128)) for t in tables]
 
     def block(r0):
         def step(z, carry):
@@ -129,14 +153,17 @@
             label = idx[z, pl.ds(pl.multiple_of(r0, 8), sub)]
             in_low = label < 128
             lane = label & 127
-            look = [jnp.where(in_low, jnp.take_along_axis(lo, lane, axis=1),
-                              jnp.take_along_axis(hi, lane, axis=1))
-                    for lo, hi in zip(low, high)]
-            w = jnp.exp2(s) * shade
-            return (acc0 + w * look[0], acc1 + w * look[1], acc2 + w * look[2], s + look[3])
+            first, second = [jnp.where(in_low, jnp.take_along_axis(lo, lane, axis=1),
+                                       jnp.take_along_axis(hi, lane, axis=1))
+                             for lo, hi in zip(low, high)]
+            codes = (first, first << 16, second, second << 16)
+            code0, code1, code2, code3 = [c.astype(jnp.float32) * g for c, g in zip(codes, spread)]
+            return (acc0 + jnp.exp2(code0 + s) * shade, acc1 + jnp.exp2(code1 + s) * shade,
+                    acc2 + jnp.exp2(code2 + s) * shade, s - jnp.exp2(code3 + sigma_middle))
 
         init = tuple(jnp.zeros((sub, cols), jnp.float32) for _ in range(4))
-        return lax.fori_loop(0, depth, step, init, unroll=True)
+        sums = lax.fori_loop(0, depth, step, init, unroll=True)
+        return tuple(a * g for a, g in zip(sums[:3], scale)) + sums[3:]
 
     def compute(d):
         tiles = [block(d * rb + sub * i) for i in range(rb // sub)]
@@ -186,9 +213,13 @@
     return pl.pallas_call(
         functools.partial(kernel, n, m),
         out_shape=jax.ShapeDtypeStruct((4, rb, cols), jnp.float32),
-        in_specs=[vm] * 3,
+        in_specs=[pl.BlockSpec(memory_space=pltpu.HBM)] * 3,
         out_specs=vm,
         scratch_shapes=[
+            pltpu.VMEM(volume.shape, volume.dtype),
+            pltpu.VMEM(tf_index.shape, tf_index.dtype),
+            pltpu.VMEM(tf_table.shape, tf_table.dtype),
+            pltpu.SemaphoreType.DMA((3,)),
             pltpu.VMEM((depth + 2, rows + 2 * PAD, cols), jnp.float32),
             pltpu.VMEM((depth, rows, cols), jnp.float32),
             pltpu.VMEM((n, 4 * rb, cols), jnp.bfloat16),

time: 22.3 us -> 20.1 us (0.901)
  Pallas kernels: 17.8 us -> 15.8 us
    pallas_call x1, Pallas kernels: 17.8 us -> 15.8 us  [on_device(): pl.pallas_call(functools.partial(kernel, n, m), out_shape=jax.ShapeDtypeS...]
where the time goes in v3:
time: 20.1 us; the launch traced here: 19.9 us
  Pallas kernels  15.8 us (79%)
  local copies, waits for them, and re-layouts  4.13 us (21%)
    pallas_call x1, Pallas kernels, on_device(): pl.pallas_call(functools.partial(kernel, n, m), out_shape=jax.ShapeDtypeS...  15.8 us
    unnamed x7, local copies, waits for them, and re-layouts  4.13 us

profile of v3, /device:TPU:0, one launch (start us, length us, event | category | flops | bytes accessed | tf_op | source)
XLA Modules:
  0.0 19.9 jit_solution(14992082631416044919)
XLA Ops:
  0.0 0.0 copy-start
  0.0 1.6 %copy-done = s32[16,256,128]{2,1,0:T(8,128)S(1)} copy-done((s32[16,256,128]{2,1,0:T(8,128)S(1)}, s32[16,256,128]{2,1,0:T(8,128)}, u32[]{:S(2)}) %copy-start) | copy-done | bytes 2097176
  1.6 0.0 copy-start.1
  1.6 1.2 %copy-done.1 = bf16[16,256,128]{2,1,0:T(8,128)(2,1)S(1)} copy-done((bf16[16,256,128]{2,1,0:T(8,128)(2,1)S(1)}, bf16[16,256,128]{2,1,0:T(8,128)(2,1)}, u32[]{:S(2)}) %copy-start.1) | copy-done | bytes 1048600
  2.8 0.0 copy-start.2
  2.8 0.7 %copy-done.2 = bf16[4,256]{1,0:T(4,128)(2,1)S(1)} copy-done((bf16[4,256]{1,0:T(4,128)(2,1)S(1)}, bf16[4,256]{1,0:T(4,128)(2,1)}, u32[]{:S(2)}) %copy-start.2) | copy-done | bytes 2072
  3.5 15.8 %shard_map.37 = f32[4,32,128]{2,1,0:T(8,128)S(1)} custom-call(bf16[16,256,128]{2,1,0:T(8,128)(2,1)S(1)} %copy-done.1, s32[16,256,128]{2,1,0:T(8,128)S(1)} %copy-done, bf16[4,256]{1,0:T(4,128)(2,1)S(1)} %copy-done.2), custom_call_target="tpu_custom_call" | custom-call | tf_op jit(solution)/shard_map/pallas_call | solution.py:213
  19.3 0.6 %copy.5 = f32[4,32,128]{2,1,0:T(8,128)} copy(f32[4,32,128]{2,1,0:T(8,128)S(1)} %shard_map.37) | data formatting | bytes 131072
Async XLA Ops:
  0.0 1.6 %copy-start = (s32[16,256,128]{2,1,0:T(8,128)S(1)}, s32[16,256,128]{2,1,0:T(8,128)}, u32[]{:S(2)}) copy-start(s32[16,256,128]{2,1,0:T(8,128)} %idx_hbm.1) | copy-start | bytes 6291460
  1.6 1.2 %copy-start.1 = (bf16[16,256,128]{2,1,0:T(8,128)(2,1)S(1)}, bf16[16,256,128]{2,1,0:T(8,128)(2,1)}, u32[]{:S(2)}) copy-start(bf16[16,256,128]{2,1,0:T(8,128)(2,1)} %vol_hbm.1) | copy-start | bytes 3145732
  2.8 0.7 %copy-start.2 = (bf16[4,256]{1,0:T(4,128)(2,1)S(1)}, bf16[4,256]{1,0:T(4,128)(2,1)}, u32[]{:S(2)}) copy-start(bf16[4,256]{1,0:T(4,128)(2,1)} %table_hbm.1) | copy-start | bytes 6148

commit v4 on v3

--- a/solution.py
+++ b/solution.py
@@ -18,7 +18,7 @@
     return jnp.where(x < 0.125, series, 1.0 - jnp.exp(-x))
 
 
-def kernel(n, m, vol_hbm, idx_hbm, table_hbm, out, vol, idx, table, load_sem, fvol, dx, part, recv, edge, zlo, zhi, from_left, from_right,
+def kernel(n, m, vol_hbm, idx_hbm, table_hbm, out, vol, idx, table, load_sem, pre, fvol, dx, part, recv, edge, zlo, zhi, from_left, from_right,
            send_sem, recv_sem, halo_send, halo_recv):
     depth, rows, cols = vol.shape
     rb = rows // n
@@ -104,7 +104,7 @@
         at = at + jnp.where((r_i == 0) & (c_i == depth + z), 1.0, 0.0)
         return total + jnp.dot(vol[z], at.astype(jnp.bfloat16), preferred_element_type=jnp.float32)
 
-    edges = lax.fori_loop(0, depth, pick, jnp.zeros((rows, cols), jnp.float32), unroll=4)
+    edges = lax.fori_loop(0, depth, pick, jnp.zeros((rows, cols), jnp.float32), unroll=True)
     edge[...] = edges.astype(jnp.bfloat16)
     neighbours = (mine > 0).astype(jnp.int32) + (mine < m - 1).astype(jnp.int32)
     pl.semaphore_wait(barrier, n - 1 + neighbours)
@@ -112,14 +112,28 @@
 
     send(along_x)
 
+    def search(word, z, r0):
+        label = idx[z, pl.ds(r0, sub)]
+        lane = label & 127
+        return jnp.where(label < 128, jnp.take_along_axis(low[word], lane, axis=1),
+                         jnp.take_along_axis(high[word], lane, axis=1))
+
+    loads[2].wait()
+
     def widen(z, c):
+        def rows_of(i, c):
+            r0 = pl.multiple_of(i * sub, sub)
+            pre[z, pl.ds(r0, sub)] = search(0, z, r0)
+            return c
+
+        lax.fori_loop(0, rows // sub, rows_of, 0, unroll=True)
         v = vol[z]
         fvol[z + 1, :PAD] = zero
         fvol[z + 1, PAD + rows:] = zero
         fvol[z + 1, PAD:PAD + rows] = v.astype(jnp.float32)
         return c
 
-    lax.fori_loop(0, depth, widen, 0, unroll=2)
+    lax.fori_loop(0, depth, widen, 0)
     receive(along_x)
     lane = lax.broadcasted_iota(jnp.int32, (rows, cols), 1)
     halo = jnp.where(lane < depth, from_left[...].astype(jnp.float32), from_right[...].astype(jnp.float32))
@@ -134,9 +148,8 @@
         dx[z] = jnp.dot(both, weights, preferred_element_type=jnp.float32)
         return c
 
-    lax.fori_loop(0, depth, stage, 0, unroll=4)
+    lax.fori_loop(0, depth, stage, 0, unroll=8)
     receive(along_z)
-    loads[2].wait()
     fvol[0, PAD:PAD + rows] = zlo[...].astype(jnp.float32)
     fvol[depth + 1, PAD:PAD + rows] = zhi[...].astype(jnp.float32)
 
@@ -150,12 +163,8 @@
             facing = gx * LIGHT[0] + gy * LIGHT[1] + gz * LIGHT[2]
             inv = lax.rsqrt(gx * gx + gy * gy + (gz * gz + 4.0))
             shade = 0.25 + jnp.abs(facing) * inv
-            label = idx[z, pl.ds(pl.multiple_of(r0, 8), sub)]
-            in_low = label < 128
-            lane = label & 127
-            first, second = [jnp.where(in_low, jnp.take_along_axis(lo, lane, axis=1),
-                                       jnp.take_along_axis(hi, lane, axis=1))
-                             for lo, hi in zip(low, high)]
+            r1 = pl.multiple_of(r0, 8)
+            first, second = pre[z, pl.ds(r1, sub)], search(1, z, r1)
             codes = (first, first << 16, second, second << 16)
             code0, code1, code2, code3 = [c.astype(jnp.float32) * g for c, g in zip(codes, spread)]
             return (acc0 + jnp.exp2(code0 + s) * shade, acc1 + jnp.exp2(code1 + s) * shade,
@@ -220,6 +229,7 @@
             pltpu.VMEM(tf_index.shape, tf_index.dtype),
             pltpu.VMEM(tf_table.shape, tf_table.dtype),
             pltpu.SemaphoreType.DMA((3,)),
+            pltpu.VMEM(tf_index.shape, jnp.int32),
             pltpu.VMEM((depth + 2, rows + 2 * PAD, cols), jnp.float32),
             pltpu.VMEM((depth, rows, cols), jnp.float32),
             pltpu.VMEM((n, 4 * rb, cols), jnp.bfloat16),
@@ -231,7 +241,7 @@
             pltpu.SemaphoreType.DMA((4,)),
         ],
         compiler_params=pltpu.CompilerParams(
-            collective_id=0, has_side_effects=True, vmem_limit_bytes=32 * 1024 * 1024),
+            collective_id=0, has_side_effects=True, vmem_limit_bytes=62 * 1024 * 1024),
     )(volume, tf_index, tf_table)
 
 

time: 20.1 us -> 16.6 us (0.83)
  local copies, waits for them, and re-layouts: 4.13 us -> 1.47 us
  Pallas kernels: 15.8 us -> 15 us
    unnamed x7 -> x1, local copies, waits for them, and re-layouts: 4.13 us -> 1.47 us
    pallas_call x1, Pallas kernels: 15.8 us -> 15 us  [on_device(): pl.pallas_call(functools.partial(kernel, n, m), out_shape=jax.ShapeDtypeS...]
where the time goes in v4:
time: 16.6 us; the launch traced here: 16.4 us
  Pallas kernels  15 us (90%)
  local copies, waits for them, and re-layouts  1.47 us (9%)
    pallas_call x1, Pallas kernels, on_device(): pl.pallas_call(functools.partial(kernel, n, m), out_shape=jax.ShapeDtypeS...  15 us
    unnamed x1, local copies, waits for them, and re-layouts  1.47 us

profile of v4, /device:TPU:0, one launch (start us, length us, event | category | flops | bytes accessed | tf_op | source)
XLA Modules:
  0.0 16.4 jit_solution(3461896092972962302)
XLA Ops:
  0.0 15.0 %shard_map.37 = f32[4,32,128]{2,1,0:T(8,128)} custom-call(bf16[16,256,128]{2,1,0:T(8,128)(2,1)} %vol_hbm.1, s32[16,256,128]{2,1,0:T(8,128)} %idx_hbm.1, bf16[4,256]{1,0:T(4,128)(2,1)} %table_hbm.1), custom_call_target="tpu_custom_call" | custom-call | tf_op jit(solution)/shard_map/pallas_call | solution.py:222
  15.0 1.5 %copy.5 = f32[4,32,128]{2,1,0:T(8,128)} copy(f32[4,32,128]{2,1,0:T(8,128)} %shard_map.37) | data formatting | bytes 131072

commit v5 on v4

--- a/solution.py
+++ b/solution.py
@@ -105,7 +105,12 @@
         return total + jnp.dot(vol[z], at.astype(jnp.bfloat16), preferred_element_type=jnp.float32)
 
     edges = lax.fori_loop(0, depth, pick, jnp.zeros((rows, cols), jnp.float32), unroll=True)
-    edge[...] = edges.astype(jnp.bfloat16)
+    fold = cols // (2 * depth)
+    short = rows // fold
+    packed = edges[:short]
+    for i in range(1, fold):
+        packed = packed + pltpu.roll(edges[i * short:(i + 1) * short], 2 * depth * i, 1)
+    edge[...] = packed.astype(jnp.bfloat16)
     neighbours = (mine > 0).astype(jnp.int32) + (mine < m - 1).astype(jnp.int32)
     pl.semaphore_wait(barrier, n - 1 + neighbours)
     send(along_z)
@@ -120,13 +125,18 @@
 
     loads[2].wait()
 
+    early = depth * 12 // 16
+
     def widen(z, c):
         def rows_of(i, c):
             r0 = pl.multiple_of(i * sub, sub)
             pre[z, pl.ds(r0, sub)] = search(0, z, r0)
             return c
 
-        lax.fori_loop(0, rows // sub, rows_of, 0, unroll=True)
+        @pl.when(z < early)
+        def _():
+            lax.fori_loop(0, rows // sub, rows_of, 0, unroll=True)
+
         v = vol[z]
         fvol[z + 1, :PAD] = zero
         fvol[z + 1, PAD + rows:] = zero
@@ -135,9 +145,11 @@
 
     lax.fori_loop(0, depth, widen, 0)
     receive(along_x)
-    lane = lax.broadcasted_iota(jnp.int32, (rows, cols), 1)
-    halo = jnp.where(lane < depth, from_left[...].astype(jnp.float32), from_right[...].astype(jnp.float32))
-    halo = halo.astype(jnp.bfloat16)
+    lane = lax.broadcasted_iota(jnp.int32, (short, cols), 1)
+    packed = jnp.where(lax.rem(lane, 2 * depth) < depth, from_left[...].astype(jnp.float32),
+                       from_right[...].astype(jnp.float32))
+    halo = [packed] + [pltpu.roll(packed, cols - 2 * depth * i, 1) for i in range(1, fold)]
+    halo = jnp.concatenate(halo, 0).astype(jnp.bfloat16)
 
     def stage(z, c):
         v = vol[z]
@@ -154,7 +166,7 @@
     fvol[depth + 1, PAD:PAD + rows] = zhi[...].astype(jnp.float32)
 
     def block(r0):
-        def step(z, carry):
+        def step(z, carry, known):
             acc0, acc1, acc2, s = carry
             at = pl.multiple_of(PAD + r0, 8)
             gx = dx[z, pl.ds(pl.multiple_of(r0, 8), sub)]
@@ -164,14 +176,16 @@
             inv = lax.rsqrt(gx * gx + gy * gy + (gz * gz + 4.0))
             shade = 0.25 + jnp.abs(facing) * inv
             r1 = pl.multiple_of(r0, 8)
-            first, second = pre[z, pl.ds(r1, sub)], search(1, z, r1)
+            first = pre[z, pl.ds(r1, sub)] if known else search(0, z, r1)
+            second = search(1, z, r1)
             codes = (first, first << 16, second, second << 16)
             code0, code1, code2, code3 = [c.astype(jnp.float32) * g for c, g in zip(codes, spread)]
             return (acc0 + jnp.exp2(code0 + s) * shade, acc1 + jnp.exp2(code1 + s) * shade,
                     acc2 + jnp.exp2(code2 + s) * shade, s - jnp.exp2(code3 + sigma_middle))
 
         init = tuple(jnp.zeros((sub, cols), jnp.float32) for _ in range(4))
-        sums = lax.fori_loop(0, depth, step, init, unroll=True)
+        sums = lax.fori_loop(0, early, functools.partial(step, known=True), init, unroll=True)
+        sums = lax.fori_loop(early, depth, functools.partial(step, known=False), sums, unroll=True)
         return tuple(a * g for a, g in zip(sums[:3], scale)) + sums[3:]
 
     def compute(d):
@@ -234,7 +248,9 @@
             pltpu.VMEM((depth, rows, cols), jnp.float32),
             pltpu.VMEM((n, 4 * rb, cols), jnp.bfloat16),
             pltpu.VMEM((n, 4 * rb, cols), jnp.bfloat16),
-            *[pltpu.VMEM((rows, cols), jnp.bfloat16)] * 5,
+            pltpu.VMEM((2 * rows * depth // cols, cols), jnp.bfloat16),
+            *[pltpu.VMEM((rows, cols), jnp.bfloat16)] * 2,
+            *[pltpu.VMEM((2 * rows * depth // cols, cols), jnp.bfloat16)] * 2,
             pltpu.SemaphoreType.DMA((n - 1,)),
             pltpu.SemaphoreType.DMA((n - 1,)),
             pltpu.SemaphoreType.DMA((4,)),

time: 16.6 us -> 16.3 us (0.982)
  Pallas kernels: 15 us -> 14.7 us
    pallas_call x1, Pallas kernels: 15 us -> 14.7 us  [on_device(): pl.pallas_call(functools.partial(kernel, n, m), out_shape=jax.ShapeDtypeS...]
where the time goes in v5:
time: 16.3 us; the launch traced here: 16.1 us
  Pallas kernels  14.7 us (90%)
  local copies, waits for them, and re-layouts  1.47 us (9%)
    pallas_call x1, Pallas kernels, on_device(): pl.pallas_call(functools.partial(kernel, n, m), out_shape=jax.ShapeDtypeS...  14.7 us
    unnamed x1, local copies, waits for them, and re-layouts  1.47 us

profile of v5, /device:TPU:0, one launch (start us, length us, event | category | flops | bytes accessed | tf_op | source)
XLA Modules:
  0.0 16.1 jit_solution(2320948829796778808)
XLA Ops:
  0.0 14.7 %shard_map.37 = f32[4,32,128]{2,1,0:T(8,128)} custom-call(bf16[16,256,128]{2,1,0:T(8,128)(2,1)} %vol_hbm.1, s32[16,256,128]{2,1,0:T(8,128)} %idx_hbm.1, bf16[4,256]{1,0:T(4,128)(2,1)} %table_hbm.1), custom_call_target="tpu_custom_call" | custom-call | tf_op jit(solution)/shard_map/pallas_call | solution.py:236
  14.7 1.5 %copy.5 = f32[4,32,128]{2,1,0:T(8,128)} copy(f32[4,32,128]{2,1,0:T(8,128)} %shard_map.37) | data formatting | bytes 131072

commit v6 on v5

--- a/solution.py
+++ b/solution.py
@@ -66,6 +66,31 @@
             @pl.when(jnp.logical_not(receives))
             def _():
                 landed[...] = jnp.zeros_like(landed)
+
+    loads[1].wait()
+    r_i = lax.broadcasted_iota(jnp.int32, (cols, cols), 0)
+    c_i = lax.broadcasted_iota(jnp.int32, (cols, cols), 1)
+    diff = jnp.where(r_i == c_i + 1, 1.0, 0.0) - jnp.where(r_i == c_i - 1, 1.0, 0.0)
+    diff = diff.astype(jnp.bfloat16)
+    zero = jnp.zeros((PAD, cols), jnp.float32)
+
+    def pick(z, total):
+        at = jnp.where((r_i == cols - 1) & (c_i == z), 1.0, 0.0)
+        at = at + jnp.where((r_i == 0) & (c_i == depth + z), 1.0, 0.0)
+        return total + jnp.dot(vol[z], at.astype(jnp.bfloat16), preferred_element_type=jnp.float32)
+
+    edges = lax.fori_loop(0, depth, pick, jnp.zeros((rows, cols), jnp.float32), unroll=True)
+    fold = cols // (2 * depth)
+    short = rows // fold
+    packed = edges[:short]
+    for i in range(1, fold):
+        packed = packed + pltpu.roll(edges[i * short:(i + 1) * short], 2 * depth * i, 1)
+    edge[...] = packed.astype(jnp.bfloat16)
+    neighbours = (mine > 0).astype(jnp.int32) + (mine < m - 1).astype(jnp.int32)
+    pl.semaphore_wait(barrier, n - 1 + neighbours)
+    send(along_z)
+
+    send(along_x)
 
     loads[0].wait()
     entries = table[...].astype(jnp.float32)
@@ -91,31 +116,6 @@
     spread = [jnp.broadcast_to(g * (1.0 / 65536.0), (sub, cols)) for g in grain]
     sigma_middle = jnp.broadcast_to(middle[3], (sub, cols))
     scale = [jnp.broadcast_to(jnp.exp2(o), (sub, cols)) for o in middle[:3]]
-
-    loads[1].wait()
-    r_i = lax.broadcasted_iota(jnp.int32, (cols, cols), 0)
-    c_i = lax.broadcasted_iota(jnp.int32, (cols, cols), 1)
-    diff = jnp.where(r_i == c_i + 1, 1.0, 0.0) - jnp.where(r_i == c_i - 1, 1.0, 0.0)
-    diff = diff.astype(jnp.bfloat16)
-    zero = jnp.zeros((PAD, cols), jnp.float32)
-
-    def pick(z, total):
-        at = jnp.where((r_i == cols - 1) & (c_i == z), 1.0, 0.0)
-        at = at + jnp.where((r_i == 0) & (c_i == depth + z), 1.0, 0.0)
-        return total + jnp.dot(vol[z], at.astype(jnp.bfloat16), preferred_element_type=jnp.float32)
-
-    edges = lax.fori_loop(0, depth, pick, jnp.zeros((rows, cols), jnp.float32), unroll=True)
-    fold = cols // (2 * depth)
-    short = rows // fold
-    packed = edges[:short]
-    for i in range(1, fold):
-        packed = packed + pltpu.roll(edges[i * short:(i + 1) * short], 2 * depth * i, 1)
-    edge[...] = packed.astype(jnp.bfloat16)
-    neighbours = (mine > 0).astype(jnp.int32) + (mine < m - 1).astype(jnp.int32)
-    pl.semaphore_wait(barrier, n - 1 + neighbours)
-    send(along_z)
-
-    send(along_x)
 
     def search(word, z, r0):
         label = idx[z, pl.ds(r0, sub)]

time: 16.3 us -> 16.3 us (level)
  no operation moved by 1% of the time
where the time goes in v6:
time: 16.3 us; the launch traced here: 16.2 us
  Pallas kernels  14.7 us (90%)
  local copies, waits for them, and re-layouts  1.47 us (9%)
    pallas_call x1, Pallas kernels, on_device(): pl.pallas_call(functools.partial(kernel, n, m), out_shape=jax.ShapeDtypeS...  14.7 us
    unnamed x1, local copies, waits for them, and re-layouts  1.47 us

profile of v6, /device:TPU:0, one launch (start us, length us, event | category | flops | bytes accessed | tf_op | source)
XLA Modules:
  0.0 16.2 jit_solution(10602455825211123881)
XLA Ops:
  0.0 14.7 %shard_map.37 = f32[4,32,128]{2,1,0:T(8,128)} custom-call(bf16[16,256,128]{2,1,0:T(8,128)(2,1)} %vol_hbm.1, s32[16,256,128]{2,1,0:T(8,128)} %idx_hbm.1, bf16[4,256]{1,0:T(4,128)(2,1)} %table_hbm.1), custom_call_target="tpu_custom_call" | custom-call | tf_op jit(solution)/shard_map/pallas_call | solution.py:236
  14.7 1.5 %copy.5 = f32[4,32,128]{2,1,0:T(8,128)} copy(f32[4,32,128]{2,1,0:T(8,128)} %shard_map.37) | data formatting | bytes 131072
